TPU v7x, 32 devices: a whole 2x2x4 slice. The times are simulated.
32 devices in a mesh: ens: 2 (over y), sfc: 4 (over z), lev: 2 (over x), trc: 2 (over core).
Axes of the slice: x: 2, y: 2, z: 4, core: 2. Of those that a mesh axis runs over, the one named last changes fastest.
Arguments:
- tracers: float32 [16, 16, 16, 4096], P('trc', 'lev', None, ('ens', 'sfc')), parts along dimension 3, may hold values from 0.2 to 2
- velocity: float32 [16, 2, 16, 4096], P('lev', None, None, ('ens', 'sfc')), parts along dimension 3, may hold values from -4 to 4
- node_mass: float32 [16, 2048], P(None, 'sfc'), may hold values from 0.25 to 4
- inverse_mass: float32 [16, 2048], P(None, 'sfc'), may hold values from 0.02 to 4, as said below
- edge_slots: int32 [4, 2048], P(None, 'sfc'), may hold values from 0 to 767, as said below
- send_rows: int32 [2, 512], P(None, 'sfc'), may hold values from 0 to 511, as said below
- land_water: float32 [16, 8192], P('trc', ('ens', 'sfc')), parts along dimension 1, may hold values from 0.1 to 3
- evap_factor: float32 [4096], P('sfc'), may hold values from 0.1 to 1
- land_counts: int32 [4], P('sfc'), may hold values from 256 to 1024, as said below
- land_slot: int32 [4, 4, 128], P('sfc'), may hold values from 0 to 1023, as said below
- atmos_node: int32 [4, 4, 128], P('sfc'), may hold values from 0 to 8191, as said below
- weight_to_atmos: float32 [4, 4, 128], P('sfc'), may hold values from 0 to 8, as said below
- weight_to_land: float32 [4, 4, 128], P('sfc'), may hold values from 0 to 0.4, as said below
- rain_rate: float32 [16], P('lev'), may hold values from 0.02 to 0.2
Outputs:
- tracers_out: float32 [16, 16, 16, 4096], P('trc', 'lev', None, ('ens', 'sfc')), parts along dimension 3
- land_out: float32 [16, 8192], P('trc', ('ens', 'sfc')), parts along dimension 1
There are 2 independent parts, one for each index of `ens`. A program takes and returns all parts, laid end to end along the dimension named above; an argument that names none is the same for every part. Nothing has to cross between parts.
Inputs may be any that keep to these rules, and one draw needn't show every extreme that they name: `edge_slots`: the element grid has 128 elements a row and 4 rows a partition, partitions follow one another along the curve, and it closes in both directions. Values under 512 are local positions in the same partition; then come the positions in the lower partition's list send_rows[1] and in the upper partition's list send_rows[0]. `send_rows`: row 0 holds the local positions of the partition's lowest-row elements, row 1 those of its highest-row elements, each row in an order of its own. `land_counts`: one partition has 1024 live cells. `land_slot`: each pair has 32 to 128 live entries first, the rest are 0 with weight 0; live entries name live slots. Some atmosphere partition receives 128 live entries from every land partition, and some land partition sends 128 to every atmosphere partition. `atmos_node`: the same entries seen from the atmosphere side; unused ones are 0. `weight_to_atmos`: zero exactly on unused entries. `weight_to_land`: zero exactly on unused entries. `inverse_mass`: the reciprocal of node_mass plus node_mass at the matching nodes of the element's edge neighbours.
All inputs are finite; a program needn't handle non-finite values.
Results may differ from a plain program's by a relative error of at most 0.0001.
Values sent between devices are 32-bit elements; how exact they have to be, the bound alone decides.
A program may use at most 128 MiB of HBM per device.

v0:
```python
import math

import jax
import jax.numpy as jnp
import numpy as np
from jax import lax
from jax.sharding import PartitionSpec as P

SUBSTEPS = 4


time_step = 0.03
land_step = 0.5


def with_halo(cells, sides, width):
    for axis, dim in sides:
        count = lax.axis_size(axis)
        head = lax.slice_in_dim(cells, 0, width, axis=dim)
        tail = lax.slice_in_dim(cells, cells.shape[dim] - width, cells.shape[dim], axis=dim)
        cells = jnp.concatenate(
            [
                lax.ppermute(tail, axis, [(i, (i + 1) % count) for i in range(count)]),
                cells,
                lax.ppermute(head, axis, [((i + 1) % count, i) for i in range(count)]),
            ],
            axis=dim,
        )
    return cells


def lagrange_derivative(points):
    point_count = len(points)
    matrix = np.zeros((point_count, point_count))
    for row_index in range(point_count):
        for column in range(point_count):
            if row_index != column:
                weight_row = np.prod(
                    [
                        points[row_index] - points[other_index]
                        for other_index in range(point_count)
                        if other_index != row_index
                    ]
                )
                weight_column = np.prod(
                    [
                        points[column] - points[other_index]
                        for other_index in range(point_count)
                        if other_index != column
                    ]
                )
                matrix[row_index, column] = weight_row / (
                    weight_column * (points[row_index] - points[column])
                )
        matrix[row_index, row_index] = sum(
            [
                1.0 / (points[row_index] - points[other_index])
                for other_index in range(point_count)
                if other_index != row_index
            ]
        )
    return matrix


def gll_tables():
    gll_points = np.array([-1.0, -1.0 / math.sqrt(5.0), 1.0 / math.sqrt(5.0), 1.0])
    gll_deriv = lagrange_derivative(gll_points)
    edge_nodes = np.array([[0, 1, 2, 3], [3, 7, 11, 15], [12, 13, 14, 15], [0, 4, 8, 12]])
    deriv_east = np.kron(np.eye(4), gll_deriv)
    deriv_north = np.kron(gll_deriv, np.eye(4))
    edge_place = np.eye(16)[edge_nodes.reshape(-1)].T
    return (deriv_east, deriv_north, edge_nodes, edge_place)


def shards(
    tracers,
    velocity,
    node_mass,
    inverse_mass,
    edge_slots,
    send_rows,
    land_water,
    evap_factor,
    land_counts,
    land_slot,
    atmos_node,
    weight_to_atmos,
    weight_to_land,
    rain_rate,
):
    highest = lax.Precision.HIGHEST
    deriv_east, deriv_north, edge_nodes, edge_place = gll_tables()
    tracer_count, level_count, node_count, element_count = tracers.shape
    row_width = send_rows.shape[1]
    land_slots = land_water.shape[1]
    lev_devices = lax.axis_size("lev")
    lev_rank = lax.axis_index("lev")
    bottom_flag = (lev_rank == lev_devices - 1).astype(jnp.float32)
    live_slots = (jnp.arange(land_slots, dtype=jnp.int32) < land_counts[0]).astype(jnp.float32)
    land_pick = land_slot[0]
    atmos_pick = atmos_node[0]
    weight_out = weight_to_atmos[0]
    weight_back = weight_to_land[0]
    east_matrix = jnp.asarray(deriv_east, jnp.float32)
    north_matrix = jnp.asarray(deriv_north, jnp.float32)
    place_matrix = jnp.asarray(edge_place, jnp.float32)
    evaporation = live_slots * evap_factor * land_water / (1.0 + land_water)
    tracer_width = evaporation.shape[0]
    outgoing = evaporation[:, land_pick] * weight_out[None]
    incoming = lax.all_to_all(outgoing, "sfc", split_axis=1, concat_axis=1, tiled=True)
    node_sums = jnp.zeros((tracer_width, node_count * element_count), jnp.float32)
    node_sums = node_sums.at[:, atmos_pick.reshape(-1)].add(incoming.reshape(tracer_width, -1))
    source = node_sums.reshape(tracer_width, node_count, element_count)
    source = bottom_flag * source
    tracer_field = tracers
    for substep in range(SUBSTEPS):
        tendency = jnp.einsum(
            "mn,qlne->qlme", east_matrix, velocity[:, 0][None] * tracer_field, precision=highest
        )
        tendency = tendency + jnp.einsum(
            "mn,qlne->qlme", north_matrix, velocity[:, 1][None] * tracer_field, precision=highest
        )
        advanced = tracer_field - time_step * tendency
        advanced = advanced.at[:, level_count - 1].add(time_step * source)
        weighted = node_mass * advanced
        packed = jnp.concatenate(
            [
                jnp.take(weighted[:, :, edge_nodes[0]], send_rows[0], axis=3),
                jnp.take(weighted[:, :, edge_nodes[2]], send_rows[1], axis=3),
            ],
            axis=3,
        )
        extended = with_halo(packed, (("sfc", 3),), row_width)
        lower_rim = extended[..., :row_width]
        upper_rim = extended[..., -row_width:]
        gathered = jnp.concatenate(
            [
                jnp.take(
                    jnp.concatenate(
                        [weighted[:, :, edge_nodes[(edge_side + 2) % 4]], lower_rim, upper_rim],
                        axis=3,
                    ),
                    edge_slots[edge_side],
                    axis=3,
                )
                for edge_side in range(4)
            ],
            axis=2,
        )
        tracer_field = (
            weighted + jnp.einsum("nc,qlce->qlne", place_matrix, gathered, precision=highest)
        ) * inverse_mass
    column_part = jnp.einsum("l,qlne->qne", rain_rate, tracer_field, precision=highest)
    rain_total = lax.psum(column_part, "lev")
    tracer_width = rain_total.shape[0]
    outgoing = rain_total.reshape(tracer_width, -1)[:, atmos_pick] * weight_back[None]
    incoming = lax.all_to_all(outgoing, "sfc", split_axis=1, concat_axis=1, tiled=True)
    slot_sums = jnp.zeros((tracer_width, land_slots), jnp.float32)
    precipitation = slot_sums.at[:, land_pick.reshape(-1)].add(incoming.reshape(tracer_width, -1))
    land_out = live_slots * (land_water + land_step * (precipitation - evaporation))
    return (tracer_field, land_out)


def solution(mesh):
    return jax.shard_map(
        shards,
        mesh=mesh,
        in_specs=(
            P("trc", "lev", None, ("ens", "sfc")),
            P("lev", None, None, ("ens", "sfc")),
            P(None, "sfc"),
            P(None, "sfc"),
            P(None, "sfc"),
            P(None, "sfc"),
            P("trc", ("ens", "sfc")),
            P("sfc"),
            P("sfc"),
            P("sfc", None, None),
            P("sfc", None, None),
            P("sfc", None, None),
            P("sfc", None, None),
            P("lev"),
        ),
        out_specs=(P("trc", "lev", None, ("ens", "sfc")), P("trc", ("ens", "sfc"))),
        check_vma=False,
    )
```

profile of v0, /device:TPU:0, one launch (start us, length us, event | category | flops | bytes accessed | tf_op | source)
XLA Modules:
  0.0 824.8 jit_solution(9965012205799361419)
XLA Ops:
  13.4 6.3 all-to-all-start
  28.1 5.1 scatter_custom_fusion
  44.5 4.7 copy.307
  49.2 5.5 gather_fusion.18
  64.2 5.9 copy.310
  70.1 5.5 gather_fusion.19
  92.4 7.9 copy.312
  100.3 9.5 %gather_fusion.20 = f32[512,8,8,4]{2,1,3,0:T(8,128)} fusion(f32[8,8,4,768]{1,0,3,2:T(8,128)} %copy.312, s32[1024]{0:T(1024)S(1)} %pad_clamp_fusion.6), kind=kCustom, calls=%fused_computation.1.clone | custom fusion | bytes 1050624 | tf_op jit(solution)/shard_map/jit(_take)/gather | solution.py:138
  109.8 6.5 copy.313
  116.3 7.9 copy.315
  124.2 9.5 %gather_fusion.21 = f32[512,8,8,4]{2,1,3,0:T(8,128)} fusion(f32[8,8,4,768]{1,0,3,2:T(8,128)} %copy.315, s32[1024]{0:T(1024)S(1)} %pad_clamp_fusion.4), kind=kCustom, calls=%fused_computation.9.clone | custom fusion | bytes 1050624 | tf_op jit(solution)/shard_map/jit(_take)/gather | solution.py:138
  133.7 7.2 copy.316
  141.0 7.9 copy.317
  148.9 9.5 %gather_fusion.22 = f32[512,8,8,4]{2,1,3,0:T(8,128)} fusion(f32[8,8,4,768]{1,0,3,2:T(8,128)} %copy.317, s32[1024]{0:T(1024)S(1)} %pad_clamp_fusion.3), kind=kCustom, calls=%fused_computation.10.clone | custom fusion | bytes 1050624 | tf_op jit(solution)/shard_map/jit(_take)/gather | solution.py:138
  158.3 7.3 copy.318
  165.6 7.9 copy.320
  173.5 9.5 %gather_fusion.23 = f32[512,8,8,4]{2,1,3,0:T(8,128)} fusion(f32[8,8,4,768]{1,0,3,2:T(8,128)} %copy.320, s32[1024]{0:T(1024)S(1)} %pad_clamp_fusion.1), kind=kCustom, calls=%fused_computation.11.clone | custom fusion | bytes 1050624 | tf_op jit(solution)/shard_map/jit(_take)/gather | solution.py:138
  183.0 7.4 copy.321
  212.4 5.7 gather_fusion.24
  223.0 6.3 copy.327
  229.3 5.5 gather_fusion.25
  252.8 7.9 copy.332
  260.7 9.5 %gather_fusion.27 = f32[512,8,8,4]{2,1,3,0:T(8,128)} fusion(f32[8,8,4,768]{1,0,3,2:T(8,128)} %copy.332, s32[1024]{0:T(1024)S(1)} %pad_clamp_fusion.4), kind=kCustom, calls=%fused_computation.13.clone | custom fusion | bytes 1050624 | tf_op jit(solution)/shard_map/jit(_take)/gather | solution.py:138
  270.1 7.2 copy.333
  278.6 7.9 copy.329
  286.5 9.5 %gather_fusion.26 = f32[512,8,8,4]{2,1,3,0:T(8,128)} fusion(f32[8,8,4,768]{1,0,3,2:T(8,128)} %copy.329, s32[1024]{0:T(1024)S(1)} %pad_clamp_fusion.6), kind=kCustom, calls=%fused_computation.12.clone | custom fusion | bytes 1050624 | tf_op jit(solution)/shard_map/jit(_take)/gather | solution.py:138
  296.0 7.2 copy.330
  305.2 7.9 copy.334
  313.1 9.5 %gather_fusion.28 = f32[512,8,8,4]{2,1,3,0:T(8,128)} fusion(f32[8,8,4,768]{1,0,3,2:T(8,128)} %copy.334, s32[1024]{0:T(1024)S(1)} %pad_clamp_fusion.3), kind=kCustom, calls=%fused_computation.14.clone | custom fusion | bytes 1050624 | tf_op jit(solution)/shard_map/jit(_take)/gather | solution.py:138
  322.6 7.2 copy.335
  331.8 7.9 copy.337
  339.7 9.5 %gather_fusion.29 = f32[512,8,8,4]{2,1,3,0:T(8,128)} fusion(f32[8,8,4,768]{1,0,3,2:T(8,128)} %copy.337, s32[1024]{0:T(1024)S(1)} %pad_clamp_fusion.1), kind=kCustom, calls=%fused_computation.15.clone | custom fusion | bytes 1050624 | tf_op jit(solution)/shard_map/jit(_take)/gather | solution.py:138
  349.2 7.4 copy.338
  379.2 5.7 gather_fusion.30
  389.8 5.9 copy.344
  395.7 5.5 gather_fusion.31
  419.2 8.3 %copy.351 = f32[8,8,4,768]{1,0,3,2:T(8,128)} copy(f32[8,8,4,768]{3,1,0,2:T(8,128)} %get-tuple-element.72) | data formatting | bytes 1572864 | tf_op jit(solution)/shard_map/concatenate | solution.py:139
  427.5 9.5 %gather_fusion.34 = f32[512,8,8,4]{2,1,3,0:T(8,128)} fusion(f32[8,8,4,768]{1,0,3,2:T(8,128)} %copy.351, s32[1024]{0:T(1024)S(1)} %pad_clamp_fusion.3), kind=kCustom, calls=%fused_computation.18.clone | custom fusion | bytes 1050624 | tf_op jit(solution)/shard_map/jit(_take)/gather | solution.py:138
  436.9 7.2 copy.352
  445.4 7.9 copy.349
  453.3 9.5 %gather_fusion.33 = f32[512,8,8,4]{2,1,3,0:T(8,128)} fusion(f32[8,8,4,768]{1,0,3,2:T(8,128)} %copy.349, s32[1024]{0:T(1024)S(1)} %pad_clamp_fusion.4), kind=kCustom, calls=%fused_computation.17.clone | custom fusion | bytes 1050624 | tf_op jit(solution)/shard_map/jit(_take)/gather | solution.py:138
  462.8 7.3 copy.350
  472.0 7.9 copy.346
  479.9 9.5 %gather_fusion.32 = f32[512,8,8,4]{2,1,3,0:T(8,128)} fusion(f32[8,8,4,768]{1,0,3,2:T(8,128)} %copy.346, s32[1024]{0:T(1024)S(1)} %pad_clamp_fusion.6), kind=kCustom, calls=%fused_computation.16.clone | custom fusion | bytes 1050624 | tf_op jit(solution)/shard_map/jit(_take)/gather | solution.py:138
  489.4 7.2 copy.347
  498.6 7.9 copy.354
  506.5 9.5 %gather_fusion.35 = f32[512,8,8,4]{2,1,3,0:T(8,128)} fusion(f32[8,8,4,768]{1,0,3,2:T(8,128)} %copy.354, s32[1024]{0:T(1024)S(1)} %pad_clamp_fusion.1), kind=kCustom, calls=%fused_computation.19.clone | custom fusion | bytes 1050624 | tf_op jit(solution)/shard_map/jit(_take)/gather | solution.py:138
  516.0 7.4 copy.355
  545.3 5.7 gather_fusion.36
  558.9 5.6 gather_fusion.37
  580.6 8.1 copy.368
  588.7 9.5 %gather_fusion.40 = f32[512,8,8,4]{2,1,3,0:T(8,128)} fusion(f32[8,8,4,768]{1,0,3,2:T(8,128)} %copy.368, s32[1024]{0:T(1024)S(1)} %pad_clamp_fusion.3), kind=kCustom, calls=%fused_computation.22.clone | custom fusion | bytes 1050624 | tf_op jit(solution)/shard_map/jit(_take)/gather | solution.py:138
  598.2 7.3 copy.369
  606.7 6.7 copy.366
  613.4 9.5 %gather_fusion.39 = f32[512,8,8,4]{2,1,3,0:T(8,128)} fusion(f32[8,8,4,768]{1,0,3,2:T(8,128)} %copy.366, s32[1024]{0:T(1024)S(1)} %pad_clamp_fusion.4), kind=kCustom, calls=%fused_computation.21.clone | custom fusion | bytes 1050624 | tf_op jit(solution)/shard_map/jit(_take)/gather | solution.py:138
  622.8 7.3 copy.367
  632.1 6.6 copy.363
  638.8 9.5 %gather_fusion.38 = f32[512,8,8,4]{2,1,3,0:T(8,128)} fusion(f32[8,8,4,768]{1,0,3,2:T(8,128)} %copy.363, s32[1024]{0:T(1024)S(1)} %pad_clamp_fusion.6), kind=kCustom, calls=%fused_computation.20.clone | custom fusion | bytes 1050624 | tf_op jit(solution)/shard_map/jit(_take)/gather | solution.py:138
  648.3 7.3 copy.364
  657.5 6.6 copy.371
  664.2 9.5 %gather_fusion.41 = f32[512,8,8,4]{2,1,3,0:T(8,128)} fusion(f32[8,8,4,768]{1,0,3,2:T(8,128)} %copy.371, s32[1024]{0:T(1024)S(1)} %pad_clamp_fusion.1), kind=kCustom, calls=%fused_computation.23.clone | custom fusion | bytes 1050624 | tf_op jit(solution)/shard_map/jit(_take)/gather | solution.py:138
  673.7 7.5 copy.372
  693.7 106.0 %all-reduce.2.cloned.1.call-done = f32[8,8192]{0,1:T(8,128)} async-done(((f32[8,8192]{0,1:T(8,128)}), f32[8,8192]{0,1:T(8,128)}) %all-reduce.2.cloned.1.call-update) | async-done | bytes 262160 | tf_op jit(solution)/shard_map/psum | solution.py:154
  808.3 5.6 all-to-all-done.1
  (200 shorter events, 226.9 us)
Async XLA Ops:
  7.2 680.2 %copy-start = (f32[8]{0:T(128)S(1)}, f32[8]{0:T(128)}, u32[]{:S(2)}) copy-start(f32[8]{0:T(128)} %param.90) | copy-start | bytes 100
  7.2 14.6 %copy-start.26 = (s32[4]{0:T(128)S(1)}, s32[4]{0:T(128)}, u32[]{:S(2)}) copy-start(s32[4]{0:T(128)} %constant.167) | copy-start | bytes 52
  7.2 14.8 %copy-start.25 = (s32[4]{0:T(128)S(1)}, s32[4]{0:T(128)}, u32[]{:S(2)}) copy-start(s32[4]{0:T(128)} %constant.168) | copy-start | bytes 52
  7.2 14.8 %copy-start.13 = (f32[16,16,1,1]{1,0,3,2:T(8,128)S(1)}, f32[16,16,1,1]{1,0,3,2:T(8,128)}, u32[]{:S(2)}) copy-start(f32[16,16,1,1]{1,0,3,2:T(8,128)} %constant.176) | copy-start | bytes 3076
  7.2 14.6 %copy-start.20 = (s32[1,4,128]{2,1,0:T(4,128)S(1)}, s32[1,4,128]{2,1,0:T(4,128)}, u32[]{:S(2)}) copy-start(s32[1,4,128]{2,1,0:T(4,128)} %param.87) | copy-start | bytes 6148
  7.2 14.6 %copy-start.24 = (s32[2,128]{1,0:T(2,128)S(1)}, s32[2,128]{1,0:T(2,128)}, u32[]{:S(2)}) copy-start(s32[2,128]{1,0:T(2,128)} %param.82) | copy-start | bytes 3076
  7.2 14.8 %copy-start.2 = (f32[8,8,16,512]{3,2,1,0:T(8,128)S(1)}, f32[8,8,16,512]{3,2,1,0:T(8,128)}, u32[]{:S(2)}) copy-start(f32[8,8,16,512]{3,2,1,0:T(8,128)} %param.77) | copy-start | bytes 6291460
  8.7 0.6 copy-start.15
  13.4 14.5 %all-to-all-start = ((f32[8,4,128]{2,0,1:T(8,128)}), f32[8,4,128]{2,0,1:T(8,128)S(1)}, u32[]{:S(2)}, u32[]{:S(2)}) async-start(f32[8,4,128]{2,0,1:T(8,128)} %multiply_bitcast_fusion.1), calls=%async_computation | async-start | bytes 32768 | tf_op jit(solution)/shard_map/all_to_all | solution.py:110
  19.7 780.0 %all-reduce.2.cloned.1.call-start = ((), (), s32[]{:S(2)}) async-start(), calls=%async_computation.2 | async-start | bytes 8388608 | tf_op jit(solution)/shard_map/psum | solution.py:154
  21.8 20.5 %copy-start.17 = (s32[1024]{0:T(1024)}, s32[1024]{0:T(1024)S(1)}, u32[]{:S(2)}) copy-start(s32[1024]{0:T(1024)S(1)} %pad_clamp_fusion.10) | copy-start | bytes 12292
  21.9 27.3 %copy-start.18 = (s32[1024]{0:T(1024)}, s32[1024]{0:T(1024)S(1)}, u32[]{:S(2)}) copy-start(s32[1024]{0:T(1024)S(1)} %pad_clamp_fusion.9) | copy-start | bytes 12292
  21.9 39.3 %copy-start.19 = (s32[1024]{0:T(1024)}, s32[1024]{0:T(1024)S(1)}, u32[]{:S(2)}) copy-start(s32[1024]{0:T(1024)S(1)} %pad_clamp_fusion.8) | copy-start | bytes 12292
  22.0 2.1 copy-start.12
  33.2 4.7 copy-start.9
  59.6 29.4 %collective-permute-start = (f32[8,8,4,128]{3,1,0,2:T(8,128)}, f32[8,8,4,128]{3,1,0,2:T(8,128)}, u32[]{:S(2)}, u32[]{:S(2)}) collective-permute-start(f32[8,8,4,128]{3,1,0,2:T(8,128)} %select_bitcast_fusion.23), channel_id=1, source_target_pairs={{0,4},{4,8},{8,12},{12,0},{1,5},{5,9},{9,13},{13,1},{2,6},{6,10},{... | collective-permute-start | bytes 393224 | tf_op jit(solution)/shard_map/ppermute | solution.py:23
  80.5 8.6 %collective-permute-start.1 = (f32[8,8,4,128]{3,1,0,2:T(8,128)}, f32[8,8,4,128]{3,1,0,2:T(8,128)}, u32[]{:S(2)}, u32[]{:S(2)}) collective-permute-start(f32[8,8,4,128]{3,1,0,2:T(8,128)} %select_bitcast_fusion.22), channel_id=1, source_target_pairs={{4,0},{8,4},{12,8},{0,12},{5,1},{9,5},{13,9},{1,13},{6,2},{10,6},{... | collective-permute-start | bytes 393224 | tf_op jit(solution)/shard_map/ppermute | solution.py:25
  190.4 1.5 copy-start.7
  190.4 1.5 copy-start.8
  190.4 1.7 copy-start.10
  190.4 1.7 copy-start.11
  223.0 26.5 %collective-permute-start.2 = (f32[8,8,4,128]{3,1,0,2:T(8,128)}, f32[8,8,4,128]{3,1,0,2:T(8,128)}, u32[]{:S(2)}, u32[]{:S(2)}) collective-permute-start(f32[8,8,4,128]{3,1,0,2:T(8,128)} %select_bitcast_fusion.21), channel_id=1, source_target_pairs={{0,4},{4,8},{8,12},{12,0},{1,5},{5,9},{9,13},{13,1},{2,6},{6,10},{... | collective-permute-start | bytes 393224 | tf_op jit(solution)/shard_map/ppermute | solution.py:23
  239.7 9.8 %collective-permute-start.3 = (f32[8,8,4,128]{3,1,0,2:T(8,128)}, f32[8,8,4,128]{3,1,0,2:T(8,128)}, u32[]{:S(2)}, u32[]{:S(2)}) collective-permute-start(f32[8,8,4,128]{3,1,0,2:T(8,128)} %select_bitcast_fusion.20), channel_id=1, source_target_pairs={{4,0},{8,4},{12,8},{0,12},{5,1},{9,5},{13,9},{1,13},{6,2},{10,6},{... | collective-permute-start | bytes 393224 | tf_op jit(solution)/shard_map/ppermute | solution.py:25
  389.8 26.1 %collective-permute-start.4 = (f32[8,8,4,128]{3,1,0,2:T(8,128)}, f32[8,8,4,128]{3,1,0,2:T(8,128)}, u32[]{:S(2)}, u32[]{:S(2)}) collective-permute-start(f32[8,8,4,128]{3,1,0,2:T(8,128)} %select_bitcast_fusion.19), channel_id=1, source_target_pairs={{0,4},{4,8},{8,12},{12,0},{1,5},{5,9},{9,13},{13,1},{2,6},{6,10},{... | collective-permute-start | bytes 393224 | tf_op jit(solution)/shard_map/ppermute | solution.py:23
  406.1 9.8 %collective-permute-start.5 = (f32[8,8,4,128]{3,1,0,2:T(8,128)}, f32[8,8,4,128]{3,1,0,2:T(8,128)}, u32[]{:S(2)}, u32[]{:S(2)}) collective-permute-start(f32[8,8,4,128]{3,1,0,2:T(8,128)} %select_bitcast_fusion.18), channel_id=1, source_target_pairs={{4,0},{8,4},{12,8},{0,12},{5,1},{9,5},{13,9},{1,13},{6,2},{10,6},{... | collective-permute-start | bytes 393224 | tf_op jit(solution)/shard_map/ppermute | solution.py:25
  554.2 23.3 %collective-permute-start.6 = (f32[8,8,4,128]{3,1,0,2:T(8,128)}, f32[8,8,4,128]{3,1,0,2:T(8,128)S(1)}, u32[]{:S(2)}, u32[]{:S(2)}) collective-permute-start(f32[8,8,4,128]{3,1,0,2:T(8,128)} %select_bitcast_fusion.17), channel_id=1, source_target_pairs={{0,4},{4,8},{8,12},{12,0},{1,5},{5,9},{9,13},{13,1},{2,6},{6,10},{... | collective-permute-start | bytes 393224 | tf_op jit(solution)/shard_map/ppermute | solution.py:23
  558.9 12.7 %copy-start.21 = (s32[1,4,128]{2,1,0:T(4,128)S(1)}, s32[1,4,128]{2,1,0:T(4,128)}, u32[]{:S(2)}) copy-start(s32[1,4,128]{2,1,0:T(4,128)} %param.87) | copy-start | bytes 6148
  567.8 9.8 %collective-permute-start.7 = (f32[8,8,4,128]{3,1,0,2:T(8,128)}, f32[8,8,4,128]{3,1,0,2:T(8,128)S(1)}, u32[]{:S(2)}, u32[]{:S(2)}) collective-permute-start(f32[8,8,4,128]{3,1,0,2:T(8,128)} %select_bitcast_fusion.16), channel_id=1, source_target_pairs={{4,0},{8,4},{12,8},{0,12},{5,1},{9,5},{13,9},{1,13},{6,2},{10,6},{... | collective-permute-start | bytes 393224 | tf_op jit(solution)/shard_map/ppermute | solution.py:25
  598.2 8.5 %copy-start.5 = (f32[8,8,4,768]{3,1,0,2:T(8,128)S(1)}, f32[8,8,4,768]{3,1,0,2:T(8,128)}, u32[]{:S(2)}) copy-start(f32[8,8,4,768]{3,1,0,2:T(8,128)} %get-tuple-element.67) | copy-start | bytes 2359300
  622.8 9.3 %copy-start.4 = (f32[8,8,4,768]{3,1,0,2:T(8,128)S(1)}, f32[8,8,4,768]{3,1,0,2:T(8,128)}, u32[]{:S(2)}) copy-start(f32[8,8,4,768]{3,1,0,2:T(8,128)} %get-tuple-element.66) | copy-start | bytes 2359300
  648.3 9.3 %copy-start.3 = (f32[8,8,4,768]{3,1,0,2:T(8,128)S(1)}, f32[8,8,4,768]{3,1,0,2:T(8,128)}, u32[]{:S(2)}) copy-start(f32[8,8,4,768]{3,1,0,2:T(8,128)} %get-tuple-element.69) | copy-start | bytes 2359300
  673.7 8.7 %copy-start.6 = (f32[8,8,4,512]{3,2,1,0:T(4,128)S(1)}, f32[8,8,4,512]{3,2,1,0:T(4,128)}, u32[]{:S(2)}) copy-start(f32[8,8,4,512]{3,2,1,0:T(4,128)} %select_bitcast_fusion.2) | copy-start | bytes 1572868
  686.0 1.3 copy-start.1
  693.1 0.7 copy-start.22
  693.1 110.0 %copy-start.23 = (f32[1,4,128]{2,1,0:T(4,128)S(1)}, f32[1,4,128]{2,1,0:T(4,128)}, u32[]{:S(2)}) copy-start(f32[1,4,128]{2,1,0:T(4,128)} %param.89) | copy-start | bytes 6148
  693.1 123.8 %copy-start.14 = (f32[8,1024]{1,0:T(8,128)S(1)}, f32[8,1024]{1,0:T(8,128)}, u32[]{:S(2)}) copy-start(f32[8,1024]{1,0:T(8,128)} %param.83) | copy-start | bytes 98308
  693.1 123.8 %copy-start.16 = (f32[1024]{0:T(1024)S(1)}, f32[1024]{0:T(1024)}, u32[]{:S(2)}) copy-start(f32[1024]{0:T(1024)} %copy-done.15) | copy-start | bytes 12292
  803.7 10.2 %all-to-all-start.1 = ((f32[8,4,128]{2,0,1:T(8,128)}), f32[8,4,128]{2,0,1:T(8,128)S(1)}, u32[]{:S(2)}, u32[]{:S(2)}) async-start(f32[8,4,128]{2,0,1:T(8,128)} %multiply_bitcast_fusion), calls=%async_computation.1 | async-start | bytes 32768 | tf_op jit(solution)/shard_map/all_to_all | solution.py:157
Sparse Core Ops, SparseCore 0:
  693.2 106.5 all-reduce.1
where the time goes:
time: 836 us; the launch traced here: 825 us
  local copies, waits for them, and re-layouts  572 us (68%)
  waiting for transfers between devices  112 us (13%)
  other arithmetic  62 us (7%)
  matrix products  36.4 us (4%)
  starting transfers between devices  26.6 us (3%)
  between operations  16.1 us (2%)
    gather x32, local copies, waits for them, and re-layouts, shards(): jnp.take(jnp.concatenate([weighted[:, :, edge_nodes[(edge_side + 2) % 4]]...  267 us
    concatenate x16, local copies, waits for them, and re-layouts, shards(): jnp.concatenate([weighted[:, :, edge_nodes[(edge_side + 2) % 4]], lower_r...  124 us
    psum x1, waiting for transfers between devices, shards(): rain_total = lax.psum(column_part, 'lev')  106 us
    gather x16, local copies, waits for them, and re-layouts, shards(): weighted[:, :, edge_nodes[(edge_side + 2) % 4]]  51.5 us
    gather x8, local copies, waits for them, and re-layouts, shards(): jnp.take(weighted[:, :, edge_nodes[2]], send_rows[1], axis=3)  35.1 us
    gather x8, local copies, waits for them, and re-layouts, shards(): jnp.take(weighted[:, :, edge_nodes[0]], send_rows[0], axis=3)  34.7 us
    gather x8, local copies, waits for them, and re-layouts, shards(): weighted[:, :, edge_nodes[0]]  34.3 us
    select_n x18, other arithmetic, shards(): jnp.take(jnp.concatenate([weighted[:, :, edge_nodes[(edge_side + 2) % 4]]...  20.6 us
  transfers between devices with their start and end apart: 11, of which 2 were waited for; matrix products, arithmetic and copies ran while one was open for 12% of the time, Pallas kernels for 0%

commit v1 on v0

v1 whole, which is shorter than its diff:
```python
import functools
import math

import jax
import jax.numpy as jnp
import numpy as np
from jax import lax
from jax.experimental import pallas as pl
from jax.experimental.pallas import tpu as pltpu
from jax.sharding import PartitionSpec as P

SUBSTEPS = 4
CHUNKS = 4
LANES = 128
time_step = 0.03
land_step = 0.5
EDGES = ((0, 1, 2, 3), (3, 7, 11, 15), (12, 13, 14, 15), (0, 4, 8, 12))
MESH = pl.DeviceIdType.MESH
F32 = jnp.float32
BF16 = jnp.bfloat16


def derivative_matrix():
    points = [-1.0, -1.0 / math.sqrt(5.0), 1.0 / math.sqrt(5.0), 1.0]
    matrix = np.zeros((4, 4))
    for i in range(4):
        for m in range(4):
            if i != m:
                w_i = np.prod([points[i] - points[o] for o in range(4) if o != i])
                w_m = np.prod([points[m] - points[o] for o in range(4) if o != m])
                matrix[i, m] = w_i / (w_m * (points[i] - points[m]))
        matrix[i, i] = sum(1.0 / (points[i] - points[o]) for o in range(4) if o != i)
    matrix[np.abs(matrix) < 1e-12] = 0.0
    return matrix


def loop(count, body, unroll_to=4):
    if count <= unroll_to:
        for i in range(count):
            body(i)
    else:
        lax.fori_loop(0, count, lambda i, c: (body(i), c)[1], 0)


def split(x):
    high = x.astype(BF16)
    low = (x - high.astype(F32)).astype(BF16)
    return jnp.concatenate([high, low], axis=0)


def fold(y):
    half = y.shape[0] // 2
    return y[:half] + y[half:]


def dot(a, b):
    return jnp.dot(a, b, preferred_element_type=F32)


def dot_t(a, b):
    return lax.dot_general(a, b, (((1,), (1,)), ((), ())), preferred_element_type=F32)


def hot(rows, first, index):
    place = lax.broadcasted_iota(jnp.int32, (rows, index.shape[1]), 0) + first
    return jnp.where(place == index, 1.0, 0.0).astype(BF16)


def kernel(
    parts,
    levs,
    tr,
    vel,
    mass,
    inv,
    slots,
    rows_sent,
    water,
    factor,
    counts,
    land_slot,
    atmos_node,
    w_out,
    w_back,
    rate,
    out,
    land,
    TS,
    W,
    VB,
    MB,
    IB,
    MS,
    OH,
    OHR,
    SOH,
    LT,
    BT,
    HL,
    G,
    RA,
    EV,
    send,
    halo,
    out_e,
    in_e,
    out_r,
    in_r,
    halo_ss,
    halo_rs,
    e_ss,
    e_rs,
    r_ss,
    r_rs,
    t_sem,
):
    N, L, Q, E = W.shape
    LC = L // CHUNKS
    R = LC * Q
    tiles = E // LANES
    land_slots = water.shape[1]
    sfc = lax.axis_index("sfc")
    lev = lax.axis_index("lev")
    group = parts * levs
    mine = lev * parts + sfc

    def peer(d):
        other = lax.rem(mine + d, group)
        return other // parts, lax.rem(other, parts)

    barrier = pltpu.get_barrier_semaphore()

    def greet(d):
        l, p = peer(d + 1)
        pl.semaphore_signal(barrier, inc=1, device_id={"sfc": p, "lev": l}, device_id_type=MESH)

    loop(group - 1, greet, 8)

    def copy_in(j):
        return pltpu.make_async_copy(
            tr.at[:, pl.ds(j * LANES, LANES)], TS.at[j], t_sem.at[j]
        )

    def copy_out(j):
        return pltpu.make_async_copy(
            TS.at[j], out.at[:, pl.ds(j * LANES, LANES)], t_sem.at[j]
        )

    for j in range(tiles):
        copy_in(j).start()

    live = jnp.where(
        lax.broadcasted_iota(jnp.int32, (1, land_slots), 1) < counts[0], 1.0, 0.0
    ).astype(F32)
    w = water[...]
    evaporation = live * factor[...] * w / (1.0 + w)
    EV[...] = evaporation
    ev2 = split(evaporation)

    def gather_land(b):
        LT[b] = hot(land_slots, 0, land_slot[pl.ds(b, 1), :])
        out_e[b] = fold(dot(ev2, LT[b])) * w_out[pl.ds(b, 1), :]

    loop(parts, gather_land)
    pl.semaphore_wait(barrier, group - 1)

    def copy_e(src, dst, p):
        return pltpu.make_async_remote_copy(
            src_ref=out_e.at[src],
            dst_ref=in_e.at[dst],
            send_sem=e_ss.at[src],
            recv_sem=e_rs.at[dst],
            device_id={"sfc": p},
            device_id_type=MESH,
        )

    def start_e(d):
        p = lax.rem(sfc + d + 1, parts)
        copy_e(p, sfc, p).start()

    loop(parts - 1, start_e)
    in_e[sfc] = out_e[sfc]

    def build_slots(i):
        k, r = i // tiles, lax.rem(i, tiles)
        first = r * LANES
        OH[k, pl.ds(pl.multiple_of(first, LANES), LANES), :] = hot(
            LANES, first, slots[pl.ds(k, 1), :]
        )

    lax.fori_loop(0, 4 * tiles, lambda i, c: (build_slots(i), c)[1], 0)
    width = rows_sent.shape[1]
    OHR[0] = hot(width, E, slots[0:1, :])
    OHR[1] = hot(width, E + width, slots[2:3, :])
    SOH[0] = hot(E, 0, rows_sent[0:1, :])
    SOH[1] = hot(E, 0, rows_sent[1:2, :])

    def build_node(b):
        node = atmos_node[pl.ds(b, 1), :]
        BT[b] = hot(E, 0, lax.rem(node, E))

    loop(parts, build_node)
    for n in range(N):
        MB[n] = jnp.broadcast_to(mass[n : n + 1, :], (Q, E))
        IB[n] = jnp.broadcast_to(inv[n : n + 1, :], (Q, E))

    def turn(i, c):
        l, j = i // tiles, lax.rem(i, tiles)
        lane = pl.ds(pl.multiple_of(j * LANES, LANES), LANES)
        for n in range(N):
            W[n, l, :, lane] = TS[j, pl.ds(l * N + n, Q, stride=L * N), :]
        for d in range(2):
            v = vel[pl.ds(pl.multiple_of((l * 2 + d) * N, N), N), lane] * time_step
            for n in range(N):
                VB[d, n, l, :, lane] = jnp.broadcast_to(v[n : n + 1], (Q, LANES))
        return c

    for j in range(tiles):
        copy_in(j).wait()
    lax.fori_loop(0, L * tiles, turn, 0)

    D = derivative_matrix()

    def advect(first):
        def one(i, c):
            l, j = first + i // tiles, lax.rem(i, tiles)
            lane = pl.ds(pl.multiple_of(j * LANES, LANES), LANES)
            t = [W[n, l, :, lane] for n in range(N)]
            f = [VB[0, n, l, :, lane] * t[n] for n in range(N)]
            acc = []
            for n in range(N):
                row, i_ = n // 4, n % 4
                terms = [float(D[i_, m]) * f[4 * row + m] for m in range(4) if D[i_, m] != 0.0]
                acc.append(functools.reduce(lambda a, b: a + b, terms))
            f = [VB[1, n, l, :, lane] * t[n] for n in range(N)]
            for n in range(N):
                row, i_ = n // 4, n % 4
                terms = [float(D[row, m]) * f[4 * m + i_] for m in range(4) if D[row, m] != 0.0]
                total = functools.reduce(lambda a, b: a + b, terms)
                W[n, l, :, lane] = MB[n, :, lane] * (t[n] - (acc[n] + total))
            return c

        lax.fori_loop(0, LC * tiles, one, 0)

    def halo_copy(s, c, d):
        other = lax.rem(sfc + (parts - 1 if d == 0 else 1), parts)
        return pltpu.make_async_remote_copy(
            src_ref=send.at[s, c, d],
            dst_ref=halo.at[s, c, d],
            send_sem=halo_ss.at[s, c, d],
            recv_sem=halo_rs.at[s, c, d],
            device_id={"sfc": other},
            device_id_type=MESH,
        )

    def emit(s, c):
        @pl.when(c == CHUNKS - 1)
        def _():
            for n in range(N):
                W[n, L - 1] = W[n, L - 1] + MS[n]

        for k in range(4):
            x = jnp.concatenate(
                [W[n, pl.ds(c * LC, LC)].reshape(R, E) for n in EDGES[k]], axis=0
            )
            HL[c, k] = split(x)
        for d in range(2):
            send[s, c, d] = fold(dot(HL[c, 2 * d], SOH[d]))
            halo_copy(s, c, d).start()

    def assemble(s, c):
        for k in range(4):
            G[k] = fold(dot(HL[c, (k + 2) % 4], OH[k]))
        for d in range(2):
            halo_copy(s, c, 1 - d).wait_recv()
            G[2 * d] = G[2 * d] + fold(dot(split(halo[s, c, 1 - d]), OHR[d]))
        for n in range(N):
            x = W[n, pl.ds(c * LC, LC)]
            for k in range(4):
                for t in range(4):
                    if EDGES[k][t] == n:
                        x = x + G[k, t * R : (t + 1) * R].reshape(LC, Q, E)
            W[n, pl.ds(c * LC, LC)] = x * IB[n][None]

    lax.fori_loop(0, CHUNKS, lambda c, x: (advect(c * LC), x)[1], 0)

    def wait_e(d):
        p = lax.rem(sfc + d + 1, parts)
        copy_e(p, p, p).wait_recv()

    loop(parts - 1, wait_e)
    MS[...] = jnp.zeros_like(MS)

    def scatter_node(a):
        where = atmos_node[pl.ds(a, 1), :] // E
        x = in_e[a]
        x = jnp.concatenate([jnp.where(where == n, x, 0.0) for n in range(N)], axis=0)
        MS[...] = MS[...] + fold(dot_t(split(x), BT[a])).reshape(N, Q, E)

    loop(parts, scatter_node)
    bottom = jnp.where(lev == levs - 1, time_step, 0.0).astype(F32)
    MS[...] = MS[...] * MB[...] * bottom
    lax.fori_loop(0, CHUNKS, lambda c, x: (emit(0, c), x)[1], 0)

    def step(i, x):
        s, c = i // CHUNKS, lax.rem(i, CHUNKS)
        assemble(s, c)
        advect(c * LC)
        emit(s + 1, c)
        return x

    lax.fori_loop(0, (SUBSTEPS - 1) * CHUNKS, step, 0)
    lax.fori_loop(0, CHUNKS, lambda c, x: (assemble(SUBSTEPS - 1, c), x)[1], 0)

    def fall(n, c):
        total = rate[0] * W[n, 0]
        for l in range(1, L):
            total = total + rate[l] * W[n, l]
        RA[n] = total
        return c

    lax.fori_loop(0, N, fall, 0)
    ra2 = split(RA[...].reshape(N * Q, E))

    def gather_node(a):
        where = atmos_node[pl.ds(a, 1), :] // E
        g = fold(dot(ra2, BT[a]))
        total = jnp.where(where == 0, g[:Q], 0.0)
        for n in range(1, N):
            total = total + jnp.where(where == n, g[n * Q : (n + 1) * Q], 0.0)
        out_r[a] = total * w_back[pl.ds(a, 1), :]

    loop(parts, gather_node)

    def copy_r(d, l, p, from_l, from_p):
        return pltpu.make_async_remote_copy(
            src_ref=out_r.at[p],
            dst_ref=in_r.at[from_l, from_p],
            send_sem=r_ss.at[d],
            recv_sem=r_rs.at[from_l, from_p],
            device_id={"sfc": p, "lev": l},
            device_id_type=MESH,
        )

    def start_r(d):
        l, p = peer(d + 1)
        copy_r(d, l, p, lev, sfc).start()

    loop(group - 1, start_r, 8)
    in_r[lev, sfc] = out_r[sfc]

    def put(i, c):
        l, j = i // tiles, lax.rem(i, tiles)
        lane = pl.ds(pl.multiple_of(j * LANES, LANES), LANES)
        for n in range(N):
            TS[j, pl.ds(l * N + n, Q, stride=L * N), :] = W[n, l, :, lane]
        return c

    lax.fori_loop(0, L * tiles, put, 0)
    for j in range(tiles):
        copy_out(j).start()

    def wait_r(d):
        l, p = peer(d + 1)
        copy_r(d, l, p, l, p).wait_recv()

    loop(group - 1, wait_r, 8)
    land[...] = jnp.zeros_like(land)

    def scatter_land(b):
        x = in_r[0, b]
        for l in range(1, levs):
            x = x + in_r[l, b]
        land[...] = land[...] + fold(dot_t(split(x), LT[b]))

    loop(parts, scatter_land)
    land[...] = live * (water[...] + land_step * (land[...] - EV[...]))

    for j in range(tiles):
        copy_out(j).wait()

    def done_e(d):
        p = lax.rem(sfc + d + 1, parts)
        copy_e(p, p, p).wait_send()

    loop(parts - 1, done_e)

    def done_r(d):
        l, p = peer(d + 1)
        copy_r(d, l, p, l, p).wait_send()

    loop(group - 1, done_r, 8)

    def done_halo(i, x):
        for d in range(2):
            halo_copy(i // CHUNKS, lax.rem(i, CHUNKS), d).wait_send()
        return x

    lax.fori_loop(0, SUBSTEPS * CHUNKS, done_halo, 0)


def shards(
    tracers,
    velocity,
    node_mass,
    inverse_mass,
    edge_slots,
    send_rows,
    land_water,
    evap_factor,
    land_counts,
    land_slot,
    atmos_node,
    weight_to_atmos,
    weight_to_land,
    rain_rate,
):
    Q, L, N, E = tracers.shape
    parts = lax.axis_size("sfc")
    levs = lax.axis_size("lev")
    width = send_rows.shape[1]
    land_slots = land_water.shape[1]
    block = land_slot.shape[2]
    R = L // CHUNKS * Q
    vmem = pl.BlockSpec(memory_space=pltpu.VMEM)
    smem = pl.BlockSpec(memory_space=pltpu.SMEM)
    specs = [vmem] * 14
    specs[0] = pl.BlockSpec(memory_space=pl.ANY)
    specs[8] = smem
    specs[13] = smem
    dma = pltpu.SemaphoreType.DMA
    tracers_out, land_out = pl.pallas_call(
        functools.partial(kernel, parts, levs),
        out_shape=(
            jax.ShapeDtypeStruct((Q * L * N, E), F32),
            jax.ShapeDtypeStruct((Q, land_slots), F32),
        ),
        in_specs=specs,
        out_specs=(pl.BlockSpec(memory_space=pl.ANY), vmem),
        scratch_shapes=[
            pltpu.VMEM((E // LANES, Q * L * N, LANES), F32),
            pltpu.VMEM((N, L, Q, E), F32),
            pltpu.VMEM((2, N, L, Q, E), F32),
            pltpu.VMEM((N, Q, E), F32),
            pltpu.VMEM((N, Q, E), F32),
            pltpu.VMEM((N, Q, E), F32),
            pltpu.VMEM((4, E, E), BF16),
            pltpu.VMEM((2, width, E), BF16),
            pltpu.VMEM((2, E, width), BF16),
            pltpu.VMEM((parts, land_slots, block), BF16),
            pltpu.VMEM((parts, E, block), BF16),
            pltpu.VMEM((CHUNKS, 4, 8 * R, E), BF16),
            pltpu.VMEM((4, 4 * R, E), F32),
            pltpu.VMEM((N, Q, E), F32),
            pltpu.VMEM((Q, land_slots), F32),
            pltpu.VMEM((SUBSTEPS, CHUNKS, 2, 4 * R, width), F32),
            pltpu.VMEM((SUBSTEPS, CHUNKS, 2, 4 * R, width), F32),
            pltpu.VMEM((parts, Q, block), F32),
            pltpu.VMEM((parts, Q, block), F32),
            pltpu.VMEM((parts, Q, block), F32),
            pltpu.VMEM((levs, parts, Q, block), F32),
            dma((SUBSTEPS, CHUNKS, 2)),
            dma((SUBSTEPS, CHUNKS, 2)),
            dma((parts,)),
            dma((parts,)),
            dma((parts * levs,)),
            dma((levs, parts)),
            dma((E // LANES,)),
        ],
        compiler_params=pltpu.CompilerParams(
            collective_id=0, has_side_effects=True, vmem_limit_bytes=56 * 1024 * 1024
        ),
    )(
        tracers.reshape(Q * L * N, E),
        velocity.reshape(-1, E),
        node_mass,
        inverse_mass,
        edge_slots,
        send_rows,
        land_water,
        evap_factor.reshape(1, -1),
        land_counts,
        land_slot[0],
        atmos_node[0],
        weight_to_atmos[0],
        weight_to_land[0],
        rain_rate,
    )
    return tracers_out.reshape(Q, L, N, E), land_out


def solution(mesh):
    return jax.shard_map(
        shards,
        mesh=mesh,
        in_specs=(
            P("trc", "lev", None, ("ens", "sfc")),
            P("lev", None, None, ("ens", "sfc")),
            P(None, "sfc"),
            P(None, "sfc"),
            P(None, "sfc"),
            P(None, "sfc"),
            P("trc", ("ens", "sfc")),
            P("sfc"),
            P("sfc"),
            P("sfc", None, None),
            P("sfc", None, None),
            P("sfc", None, None),
            P("sfc", None, None),
            P("lev"),
        ),
        out_specs=(P("trc", "lev", None, ("ens", "sfc")), P("trc", ("ens", "sfc"))),
        check_vma=False,
    )
```

time: 836 us -> 51.1 us (0.06); the launches traced: 825 us -> 50.9 us
  local copies, waits for them, and re-layouts: 572 us -> 3.85 us
  waiting for transfers between devices: 112 us -> 0 us
  other arithmetic: 62 us -> 0 us
  Pallas kernels: 0 us -> 45.8 us
  matrix products: 36.4 us -> 0 us
  starting transfers between devices: 26.6 us -> 0 us
  between operations: 16.1 us -> 1.3 us
    gather x76 -> x0, local copies, waits for them, and re-layouts: 428 us -> none  [the longest x32 267 us: shards(): jnp.take(jnp.concatenate([weighted[:, :, edge_nodes[(edge_side + 2) % 4]]...]
    concatenate x16 -> x0, local copies, waits for them, and re-layouts: 124 us -> none  [shards(): jnp.concatenate([weighted[:, :, edge_nodes[(edge_side + 2) % 4]], lower_r...]
    psum x1 -> x0, waiting for transfers between devices: 106 us -> none  [shards(): rain_total = lax.psum(column_part, 'lev')]
    pallas_call x0 -> x1, Pallas kernels: none -> 45.8 us  [shards(): pl.pallas_call(functools.partial(kernel, parts, levs), out_shape=(jax.Sha...]
    dot_general x13 -> x0, matrix products: 36.4 us -> none  [the longest x4 13.8 us: shards(): jnp.einsum('nc,qlce->qlne', place_matrix, gathered, precision=highest)]
    select_n x30 -> x0, other arithmetic: 32 us -> none  [the longest x18 20.6 us: shards(): jnp.take(jnp.concatenate([weighted[:, :, edge_nodes[(edge_side + 2) % 4]]...]
    ppermute x8 -> x0, starting transfers between devices: 15.7 us -> none  [the longest x4 14.1 us: with_halo(): lax.ppermute(head, axis, [((i + 1) % count, i) for i in range(count)])]
    concatenate x4 -> x0, other arithmetic: 12.9 us -> none  [shards(): jnp.concatenate([weighted[:, :, edge_nodes[(edge_side + 2) % 4]], lower_r...]
  transfers between devices with their start and end apart: 11 -> 0, of which waited for: 2 -> 0; matrix products, arithmetic and copies ran while one was open for 12% -> 0% of each run, Pallas kernels for 0% -> 0%
where the time goes in v1:
time: 51.1 us; the launch traced here: 50.9 us
  Pallas kernels  45.8 us (90%)
  local copies, waits for them, and re-layouts  3.85 us (8%)
  between operations  1.3 us (3%)
    pallas_call x1, Pallas kernels, shards(): pl.pallas_call(functools.partial(kernel, parts, levs), out_shape=(jax.Sha...  45.8 us
    unnamed x4, local copies, waits for them, and re-layouts  3.85 us

profile of v1, /device:TPU:0, one launch (start us, length us, event | category | flops | bytes accessed | tf_op | source)
XLA Modules:
  0.0 50.9 jit_solution(12560624991094870358)
XLA Ops:
  1.3 45.8 %shard_map.149 = (f32[1024,512]{1,0:T(8,128)}, f32[8,1024]{1,0:T(8,128)}) custom-call(f32[1024,512]{1,0:T(8,128)} %bitcast.8, f32[256,512]{1,0:T(8,128)} %bitcast.10, f32[16,512]{1,0:T(8,128)} %mass.1, f32[16,512]{1,0:T(8,128)} %inv.1, s32[4,512]{1,0:T(4,128)} %slots.1, s32[2,128]{1,0:T(2,128)} %rows_sent.1, f32[8,1024]{1,0:T(8,128)} %water.1, ...), custom_call_target="tpu_custom_call" | custom-call | tf_op jit(solution)/shard_map/pallas_call | solution.py:432
  47.0 0.0 copy-start
  47.1 3.2 %copy.19 = f32[8,8,16,512]{3,2,1,0:T(8,128)} copy(f32[8,8,16,512]{3,2,1,0:T(8,128)} %bitcast.9) | data formatting | bytes 4194304
  50.3 0.0 copy-done
  50.3 0.6 %copy.20 = f32[8,1024]{1,0:T(8,128)} copy(f32[8,1024]{1,0:T(8,128)S(1)} %copy-done) | data formatting | bytes 65536
Async XLA Ops:
  47.0 3.2 %copy-start = (f32[8,1024]{1,0:T(8,128)S(1)}, f32[8,1024]{1,0:T(8,128)}, u32[]{:S(2)}) copy-start(f32[8,1024]{1,0:T(8,128)} %get-tuple-element.9) | copy-start | bytes 98308

commit v2 on v1

--- a/solution.py
+++ b/solution.py
@@ -162,7 +162,6 @@
         out_e[b] = fold(dot(ev2, LT[b])) * w_out[pl.ds(b, 1), :]
 
     loop(parts, gather_land)
-    pl.semaphore_wait(barrier, group - 1)
 
     def copy_e(src, dst, p):
         return pltpu.make_async_remote_copy(
@@ -174,35 +173,10 @@
             device_id_type=MESH,
         )
 
-    def start_e(d):
-        p = lax.rem(sfc + d + 1, parts)
-        copy_e(p, sfc, p).start()
-
-    loop(parts - 1, start_e)
-    in_e[sfc] = out_e[sfc]
-
-    def build_slots(i):
-        k, r = i // tiles, lax.rem(i, tiles)
-        first = r * LANES
-        OH[k, pl.ds(pl.multiple_of(first, LANES), LANES), :] = hot(
-            LANES, first, slots[pl.ds(k, 1), :]
-        )
-
-    lax.fori_loop(0, 4 * tiles, lambda i, c: (build_slots(i), c)[1], 0)
-    width = rows_sent.shape[1]
-    OHR[0] = hot(width, E, slots[0:1, :])
-    OHR[1] = hot(width, E + width, slots[2:3, :])
     SOH[0] = hot(E, 0, rows_sent[0:1, :])
     SOH[1] = hot(E, 0, rows_sent[1:2, :])
-
-    def build_node(b):
-        node = atmos_node[pl.ds(b, 1), :]
-        BT[b] = hot(E, 0, lax.rem(node, E))
-
-    loop(parts, build_node)
     for n in range(N):
         MB[n] = jnp.broadcast_to(mass[n : n + 1, :], (Q, E))
-        IB[n] = jnp.broadcast_to(inv[n : n + 1, :], (Q, E))
 
     def turn(i, c):
         l, j = i // tiles, lax.rem(i, tiles)
@@ -259,14 +233,18 @@
             for n in range(N):
                 W[n, L - 1] = W[n, L - 1] + MS[n]
 
-        for k in range(4):
+        def edge(k):
             x = jnp.concatenate(
                 [W[n, pl.ds(c * LC, LC)].reshape(R, E) for n in EDGES[k]], axis=0
             )
             HL[c, k] = split(x)
+
         for d in range(2):
+            edge(2 * d)
             send[s, c, d] = fold(dot(HL[c, 2 * d], SOH[d]))
             halo_copy(s, c, d).start()
+        edge(1)
+        edge(3)
 
     def assemble(s, c):
         for k in range(4):
@@ -282,7 +260,40 @@
                         x = x + G[k, t * R : (t + 1) * R].reshape(LC, Q, E)
             W[n, pl.ds(c * LC, LC)] = x * IB[n][None]
 
-    lax.fori_loop(0, CHUNKS, lambda c, x: (advect(c * LC), x)[1], 0)
+    pl.semaphore_wait(barrier, group - 1)
+    def start_e(d):
+        p = lax.rem(sfc + d + 1, parts)
+        copy_e(p, sfc, p).start()
+
+    loop(parts - 1, start_e)
+    in_e[sfc] = out_e[sfc]
+
+    def first(c, x):
+        advect(c * LC)
+        emit(0, c)
+        return x
+
+    lax.fori_loop(0, CHUNKS - 1, first, 0)
+    def build_slots(i):
+        k, r = i // tiles, lax.rem(i, tiles)
+        first = r * LANES
+        OH[k, pl.ds(pl.multiple_of(first, LANES), LANES), :] = hot(
+            LANES, first, slots[pl.ds(k, 1), :]
+        )
+
+    lax.fori_loop(0, 4 * tiles, lambda i, c: (build_slots(i), c)[1], 0)
+    width = rows_sent.shape[1]
+    OHR[0] = hot(width, E, slots[0:1, :])
+    OHR[1] = hot(width, E + width, slots[2:3, :])
+
+    def build_node(b):
+        node = atmos_node[pl.ds(b, 1), :]
+        BT[b] = hot(E, 0, lax.rem(node, E))
+
+    loop(parts, build_node)
+    for n in range(N):
+        IB[n] = jnp.broadcast_to(inv[n : n + 1, :], (Q, E))
+    advect((CHUNKS - 1) * LC)
 
     def wait_e(d):
         p = lax.rem(sfc + d + 1, parts)
@@ -300,7 +311,7 @@
     loop(parts, scatter_node)
     bottom = jnp.where(lev == levs - 1, time_step, 0.0).astype(F32)
     MS[...] = MS[...] * MB[...] * bottom
-    lax.fori_loop(0, CHUNKS, lambda c, x: (emit(0, c), x)[1], 0)
+    emit(0, CHUNKS - 1)
 
     def step(i, x):
         s, c = i // CHUNKS, lax.rem(i, CHUNKS)

time: 51.1 us -> 49.6 us (0.971)
  Pallas kernels: 45.8 us -> 44.3 us
    pallas_call x1, Pallas kernels: 45.8 us -> 44.3 us  [shards(): pl.pallas_call(functools.partial(kernel, parts, levs), out_shape=(jax.Sha...]
where the time goes in v2:
time: 49.6 us; the launch traced here: 49.4 us
  Pallas kernels  44.3 us (89%)
  local copies, waits for them, and re-layouts  3.85 us (8%)
  between operations  1.3 us (3%)
    pallas_call x1, Pallas kernels, shards(): pl.pallas_call(functools.partial(kernel, parts, levs), out_shape=(jax.Sha...  44.3 us
    unnamed x4, local copies, waits for them, and re-layouts  3.85 us

profile of v2, /device:TPU:0, one launch (start us, length us, event | category | flops | bytes accessed | tf_op | source)
XLA Modules:
  0.0 49.4 jit_solution(13471182144480355174)
XLA Ops:
  1.3 44.3 %shard_map.149 = (f32[1024,512]{1,0:T(8,128)}, f32[8,1024]{1,0:T(8,128)}) custom-call(f32[1024,512]{1,0:T(8,128)} %bitcast.8, f32[256,512]{1,0:T(8,128)} %bitcast.10, f32[16,512]{1,0:T(8,128)} %mass.1, f32[16,512]{1,0:T(8,128)} %inv.1, s32[4,512]{1,0:T(4,128)} %slots.1, s32[2,128]{1,0:T(2,128)} %rows_sent.1, f32[8,1024]{1,0:T(8,128)} %water.1, ...), custom_call_target="tpu_custom_call" | custom-call | tf_op jit(solution)/shard_map/pallas_call | solution.py:443
  45.6 0.0 copy-start
  45.6 3.2 %copy.19 = f32[8,8,16,512]{3,2,1,0:T(8,128)} copy(f32[8,8,16,512]{3,2,1,0:T(8,128)} %bitcast.9) | data formatting | bytes 4194304
  48.8 0.0 copy-done
  48.8 0.6 %copy.20 = f32[8,1024]{1,0:T(8,128)} copy(f32[8,1024]{1,0:T(8,128)S(1)} %copy-done) | data formatting | bytes 65536
Async XLA Ops:
  45.6 3.2 %copy-start = (f32[8,1024]{1,0:T(8,128)S(1)}, f32[8,1024]{1,0:T(8,128)}, u32[]{:S(2)}) copy-start(f32[8,1024]{1,0:T(8,128)} %get-tuple-element.9) | copy-start | bytes 98308

commit v3 on v2

--- a/solution.py
+++ b/solution.py
@@ -113,6 +113,7 @@
     r_ss,
     r_rs,
     t_sem,
+    o_sem,
 ):
     N, L, Q, E = W.shape
     LC = L // CHUNKS
@@ -141,13 +142,12 @@
             tr.at[:, pl.ds(j * LANES, LANES)], TS.at[j], t_sem.at[j]
         )
 
-    def copy_out(j):
-        return pltpu.make_async_copy(
-            TS.at[j], out.at[:, pl.ds(j * LANES, LANES)], t_sem.at[j]
-        )
-
     for j in range(tiles):
         copy_in(j).start()
+
+    def copy_out(c):
+        levels = pl.ds(c * LC, LC)
+        return pltpu.make_async_copy(W.at[:, levels], out.at[:, levels], o_sem.at[c])
 
     live = jnp.where(
         lax.broadcasted_iota(jnp.int32, (1, land_slots), 1) < counts[0], 1.0, 0.0
@@ -321,7 +321,13 @@
         return x
 
     lax.fori_loop(0, (SUBSTEPS - 1) * CHUNKS, step, 0)
-    lax.fori_loop(0, CHUNKS, lambda c, x: (assemble(SUBSTEPS - 1, c), x)[1], 0)
+
+    def last(c, x):
+        assemble(SUBSTEPS - 1, c)
+        copy_out(c).start()
+        return x
+
+    lax.fori_loop(0, CHUNKS, last, 0)
 
     def fall(n, c):
         total = rate[0] * W[n, 0]
@@ -360,17 +366,6 @@
     loop(group - 1, start_r, 8)
     in_r[lev, sfc] = out_r[sfc]
 
-    def put(i, c):
-        l, j = i // tiles, lax.rem(i, tiles)
-        lane = pl.ds(pl.multiple_of(j * LANES, LANES), LANES)
-        for n in range(N):
-            TS[j, pl.ds(l * N + n, Q, stride=L * N), :] = W[n, l, :, lane]
-        return c
-
-    lax.fori_loop(0, L * tiles, put, 0)
-    for j in range(tiles):
-        copy_out(j).start()
-
     def wait_r(d):
         l, p = peer(d + 1)
         copy_r(d, l, p, l, p).wait_recv()
@@ -387,8 +382,8 @@
     loop(parts, scatter_land)
     land[...] = live * (water[...] + land_step * (land[...] - EV[...]))
 
-    for j in range(tiles):
-        copy_out(j).wait()
+    for c in range(CHUNKS):
+        copy_out(c).wait()
 
     def done_e(d):
         p = lax.rem(sfc + d + 1, parts)
@@ -408,6 +403,18 @@
         return x
 
     lax.fori_loop(0, SUBSTEPS * CHUNKS, done_halo, 0)
+
+
+def finish(w, land_in, out, land, turned):
+    N, pair, Q, E = w.shape
+    for l in range(pair):
+        for j in range(E // LANES):
+            lane = slice(j * LANES, (j + 1) * LANES)
+            for n in range(N):
+                turned[l, j, pl.ds(n, Q, stride=N), :] = w[n, l, :, lane]
+            for q in range(Q):
+                out[q, l, :, lane] = turned[l, j, q * N : (q + 1) * N, :]
+    land[...] = land_in[...]
 
 
 def shards(
@@ -440,10 +447,10 @@
     specs[8] = smem
     specs[13] = smem
     dma = pltpu.SemaphoreType.DMA
-    tracers_out, land_out = pl.pallas_call(
+    nodes_first, land_sum = pl.pallas_call(
         functools.partial(kernel, parts, levs),
         out_shape=(
-            jax.ShapeDtypeStruct((Q * L * N, E), F32),
+            jax.ShapeDtypeStruct((N, L, Q, E), F32),
             jax.ShapeDtypeStruct((Q, land_slots), F32),
         ),
         in_specs=specs,
@@ -477,6 +484,7 @@
             dma((parts * levs,)),
             dma((levs, parts)),
             dma((E // LANES,)),
+            dma((CHUNKS,)),
         ],
         compiler_params=pltpu.CompilerParams(
             collective_id=0, has_side_effects=True, vmem_limit_bytes=56 * 1024 * 1024
@@ -497,7 +505,24 @@
         weight_to_land[0],
         rain_rate,
     )
-    return tracers_out.reshape(Q, L, N, E), land_out
+    pair = math.gcd(L, 4)
+    return pl.pallas_call(
+        finish,
+        grid=(L // pair,),
+        out_shape=(
+            jax.ShapeDtypeStruct((Q, L, N, E), F32),
+            jax.ShapeDtypeStruct((Q, land_slots), F32),
+        ),
+        in_specs=[
+            pl.BlockSpec((N, pair, Q, E), lambda i: (0, i, 0, 0)),
+            pl.BlockSpec((Q, land_slots), lambda i: (0, 0)),
+        ],
+        out_specs=(
+            pl.BlockSpec((Q, pair, N, E), lambda i: (0, i, 0, 0)),
+            pl.BlockSpec((Q, land_slots), lambda i: (0, 0)),
+        ),
+        scratch_shapes=[pltpu.VMEM((pair, E // LANES, Q * N, LANES), F32)],
+    )(nodes_first, land_sum)
 
 
 def solution(mesh):

time: 49.6 us -> 48.8 us (0.984)
  local copies, waits for them, and re-layouts: 3.85 us -> 0 us
  Pallas kernels: 44.3 us -> 47.3 us
    unnamed x4 -> x0, local copies, waits for them, and re-layouts: 3.85 us -> none
    pallas_call x0 -> x1, Pallas kernels: none -> 3.02 us  [shards(): pl.pallas_call(finish, grid=(L // pair,), out_shape=(jax.ShapeDtypeStruct...]
where the time goes in v3:
time: 48.8 us; the launch traced here: 48.6 us
  Pallas kernels  47.3 us (97%)
  between operations  1.29 us (3%)
    pallas_call x1, Pallas kernels, shards(): pl.pallas_call(functools.partial(kernel, parts, levs), out_shape=(jax.Sha...  44.3 us
    pallas_call x1, Pallas kernels, shards(): pl.pallas_call(finish, grid=(L // pair,), out_shape=(jax.ShapeDtypeStruct...  3.02 us

profile of v3, /device:TPU:0, one launch (start us, length us, event | category | flops | bytes accessed | tf_op | source)
XLA Modules:
  0.0 48.6 jit_solution(8430619377059627789)
XLA Ops:
  1.3 44.3 %shard_map.149 = (f32[16,8,8,512]{3,2,1,0:T(8,128)}, f32[8,1024]{1,0:T(8,128)}) custom-call(f32[1024,512]{1,0:T(8,128)} %bitcast.7, f32[256,512]{1,0:T(8,128)} %bitcast.8, f32[16,512]{1,0:T(8,128)} %mass.1, f32[16,512]{1,0:T(8,128)} %inv.1, s32[4,512]{1,0:T(4,128)} %slots.1, s32[2,128]{1,0:T(2,128)} %rows_sent.1, f32[8,1024]{1,0:T(8,128)} %water.1, ...), custom_call_target="tpu_custom_call" | custom-call | tf_op jit(solution)/shard_map/pallas_call | solution.py:450
  45.6 3.0 %shard_map.150 = (f32[8,8,16,512]{3,2,1,0:T(8,128)}, f32[8,1024]{1,0:T(8,128)}) custom-call(f32[16,8,8,512]{3,2,1,0:T(8,128)} %get-tuple-element.4.w, f32[8,1024]{1,0:T(8,128)} %get-tuple-element.5.land_in), custom_call_target="tpu_custom_call" | custom-call | tf_op jit(solution)/shard_map/pallas_call | solution.py:509

commit v4 on v3

--- a/solution.py
+++ b/solution.py
@@ -214,7 +214,7 @@
                 W[n, l, :, lane] = MB[n, :, lane] * (t[n] - (acc[n] + total))
             return c
 
-        lax.fori_loop(0, LC * tiles, one, 0)
+        lax.fori_loop(0, LC * tiles, one, 0, unroll=2)
 
     def halo_copy(s, c, d):
         other = lax.rem(sfc + (parts - 1 if d == 0 else 1), parts)

time: 48.8 us -> 47.9 us (0.982)
  Pallas kernels: 47.3 us -> 46.4 us
    pallas_call x1, Pallas kernels: 44.3 us -> 43.4 us  [shards(): pl.pallas_call(functools.partial(kernel, parts, levs), out_shape=(jax.Sha...]
where the time goes in v4:
time: 47.9 us; the launch traced here: 47.7 us
  Pallas kernels  46.4 us (97%)
  between operations  1.29 us (3%)
    pallas_call x1, Pallas kernels, shards(): pl.pallas_call(functools.partial(kernel, parts, levs), out_shape=(jax.Sha...  43.4 us
    pallas_call x1, Pallas kernels, shards(): pl.pallas_call(finish, grid=(L // pair,), out_shape=(jax.ShapeDtypeStruct...  3.02 us

profile of v4, /device:TPU:0, one launch (start us, length us, event | category | flops | bytes accessed | tf_op | source)
XLA Modules:
  0.0 47.7 jit_solution(9351203991603889625)
XLA Ops:
  1.3 43.4 %shard_map.149 = (f32[16,8,8,512]{3,2,1,0:T(8,128)}, f32[8,1024]{1,0:T(8,128)}) custom-call(f32[1024,512]{1,0:T(8,128)} %bitcast.7, f32[256,512]{1,0:T(8,128)} %bitcast.8, f32[16,512]{1,0:T(8,128)} %mass.1, f32[16,512]{1,0:T(8,128)} %inv.1, s32[4,512]{1,0:T(4,128)} %slots.1, s32[2,128]{1,0:T(2,128)} %rows_sent.1, f32[8,1024]{1,0:T(8,128)} %water.1, ...), custom_call_target="tpu_custom_call" | custom-call | tf_op jit(solution)/shard_map/pallas_call | solution.py:450
  44.7 3.0 %shard_map.150 = (f32[8,8,16,512]{3,2,1,0:T(8,128)}, f32[8,1024]{1,0:T(8,128)}) custom-call(f32[16,8,8,512]{3,2,1,0:T(8,128)} %get-tuple-element.4.w, f32[8,1024]{1,0:T(8,128)} %get-tuple-element.5.land_in), custom_call_target="tpu_custom_call" | custom-call | tf_op jit(solution)/shard_map/pallas_call | solution.py:509
